TPU v7x, 256 devices: a whole 4x4x8 slice. The times are simulated.
256 devices in a mesh: dp: 16 (over z_lo, y), hidden: 16 (over x, z_hi, core).
Axes of the slice: x: 4, y: 4, z: 8 (z_hi: 2, z_lo: 4; z = z_hi * 4 + z_lo), core: 2. Of those that a mesh axis runs over, the one named last changes fastest.
Arguments:
- activations: bfloat16 [4, 128, 8192], P(None, 'hidden', 'dp'), may hold values from -6 to 6
- out_grad: bfloat16 [4, 128, 8192], P(None, 'hidden', 'dp'), may hold values from -6 to 6
- w_gate: bfloat16 [8192, 28672], P('dp', 'hidden'), may hold values from -0.0625 to 0.0625
- w_up: bfloat16 [8192, 28672], P('dp', 'hidden'), may hold values from -0.0625 to 0.0625
- w_down: bfloat16 [28672, 8192], P('hidden', 'dp'), may hold values from -0.03125 to 0.03125
- levels: int32 [4], replicated, may hold values from 0 to 3, each once
Outputs:
- input_grad: bfloat16 [4, 128, 8192], P(None, 'hidden', 'dp')
- gate_grad: bfloat16 [8192, 28672], P('dp', 'hidden')
- up_grad: bfloat16 [8192, 28672], P('dp', 'hidden')
- down_grad: bfloat16 [28672, 8192], P('hidden', 'dp')
Inputs may be any that keep to these rules, and one draw needn't show every extreme that they name: Each of 0 to 3 appears once; micro-batch b uses the first (3584) * 2 ** levels[b] hidden units.
All inputs are finite; a program needn't handle non-finite values.
Results may differ from a plain program's by a relative error of at most 0.005.
Values may be sent and summed in bfloat16 or wider, within the bound.
A program may use at most 128 MiB of HBM per device.

v0:
```python
import jax
import jax.numpy as jnp
from jax import lax
from jax.sharding import PartitionSpec as P


def local_units(gate_sum, up_sum, hidden_grad, level_row, unit_ids, full_width):
    limit_row = jnp.left_shift(jnp.ones_like(level_row), level_row) * (full_width // 8)
    active = unit_ids[None, :] < limit_row[:, None]
    sigmoid_gate = jax.nn.sigmoid(gate_sum)
    zero_value = jnp.zeros_like(gate_sum)
    hidden_act = jnp.where(active, gate_sum * sigmoid_gate * up_sum, zero_value).astype(
        jnp.bfloat16
    )
    masked_grad = jnp.where(active, hidden_grad, zero_value)
    dgate = (masked_grad * up_sum * sigmoid_gate * (1.0 + gate_sum * (1.0 - sigmoid_gate))).astype(
        jnp.bfloat16
    )
    dup = (masked_grad * gate_sum * sigmoid_gate).astype(jnp.bfloat16)
    return (hidden_act, dgate, dup)


def flatten_parts(parts, leading):
    return jnp.concatenate([part.reshape(leading, -1) for part in parts], axis=1)


def split_parts(packed, shapes):
    results = []
    offset = 0
    for row_total, col_total in shapes:
        span_size = row_total * col_total // packed.shape[0]
        results.append(packed[:, offset : offset + span_size].reshape(row_total, col_total))
        offset = offset + span_size
    return results


def body(activations, out_grad, w_gate, w_up, w_down, levels):
    level_count, tok_rows, features = activations.shape
    hidden_count = lax.axis_size("hidden")
    dp_count = lax.axis_size("dp")
    micro_rows = tok_rows * hidden_count
    shard_width = w_gate.shape[1]
    full_width = shard_width * hidden_count
    hidden_index = lax.axis_index("hidden")
    rows_x, rows_g = (
        lax.all_gather(activations, "hidden", axis=1, tiled=True),
        lax.all_gather(out_grad, "hidden", axis=1, tiled=True),
    )
    members = []
    row_total = level_count * micro_rows
    level_row = jnp.repeat(levels, micro_rows, total_repeat_length=row_total)
    unit_ids = hidden_index * shard_width + lax.iota(jnp.int32, shard_width)
    members.append(
        (
            0,
            rows_x.reshape(row_total, features),
            rows_g.reshape(row_total, features),
            level_row,
            unit_ids,
            w_gate,
            w_up,
            w_down,
        )
    )
    contract_units = (((1,), (1,)), ((), ()))
    contract_rows = (((0,), (0,)), ((), ()))
    gate_terms = [
        jnp.dot(member[1], member[5], preferred_element_type=jnp.float32) for member in members
    ]
    up_terms = [
        jnp.dot(member[1], member[6], preferred_element_type=jnp.float32) for member in members
    ]
    grad_terms = [
        lax.dot_general(member[2], member[7], contract_units, preferred_element_type=jnp.float32)
        for member in members
    ]
    full_shapes = [(member[1].shape[0], member[5].shape[1]) for member in members]
    gate_pack = flatten_parts(gate_terms, dp_count)
    up_pack = flatten_parts(up_terms, dp_count)
    grad_pack = flatten_parts(grad_terms, dp_count)
    gate_part, up_part, grad_part = (
        lax.psum_scatter(gate_pack, "dp", scatter_dimension=0, tiled=True),
        lax.psum_scatter(up_pack, "dp", scatter_dimension=0, tiled=True),
        lax.psum_scatter(grad_pack, "dp", scatter_dimension=0, tiled=True),
    )
    share_shapes = [(row_total // dp_count, col_total) for row_total, col_total in full_shapes]
    gate_list = split_parts(gate_part, share_shapes)
    up_list = split_parts(up_part, share_shapes)
    grad_list = split_parts(grad_part, share_shapes)
    dp_index = lax.axis_index("dp")
    position = 0
    share_rows = share_shapes[position][0]
    level_share = lax.dynamic_slice_in_dim(members[position][3], dp_index * share_rows, share_rows)
    outcome = [
        local_units(
            gate_list[position],
            up_list[position],
            grad_list[position],
            level_share,
            members[position][4],
            full_width,
        )
    ]
    act_pack = flatten_parts([entry[0] for entry in outcome], 1)
    dgate_pack = flatten_parts([entry[1] for entry in outcome], 1)
    dup_pack = flatten_parts([entry[2] for entry in outcome], 1)
    act_all, dgate_all, dup_all = (
        lax.all_gather(act_pack, "dp", axis=0, tiled=True),
        lax.all_gather(dgate_pack, "dp", axis=0, tiled=True),
        lax.all_gather(dup_pack, "dp", axis=0, tiled=True),
    )
    act_list = split_parts(act_all, full_shapes)
    dgate_list = split_parts(dgate_all, full_shapes)
    dup_list = split_parts(dup_all, full_shapes)
    input_sum = None
    position = 0
    member = members[position]
    gate_parts = lax.dot_general(
        member[1], dgate_list[position], contract_rows, preferred_element_type=jnp.float32
    ).astype(jnp.bfloat16)
    up_parts = lax.dot_general(
        member[1], dup_list[position], contract_rows, preferred_element_type=jnp.float32
    ).astype(jnp.bfloat16)
    down_parts = lax.dot_general(
        act_list[position], member[2], contract_rows, preferred_element_type=jnp.float32
    ).astype(jnp.bfloat16)
    input_term = lax.dot_general(
        dgate_list[position], member[5], contract_units, preferred_element_type=jnp.float32
    )
    input_term = input_term + lax.dot_general(
        dup_list[position], member[6], contract_units, preferred_element_type=jnp.float32
    )
    input_sum = input_term
    input_sum = input_sum.reshape(level_count, micro_rows, features)
    input_grad = lax.psum_scatter(input_sum, "hidden", scatter_dimension=1, tiled=True).astype(
        jnp.bfloat16
    )
    return (input_grad, gate_parts, up_parts, down_parts)


def solution(mesh):
    placed = (
        P(None, "hidden", "dp"),
        P(None, "hidden", "dp"),
        P("dp", "hidden"),
        P("dp", "hidden"),
        P("hidden", "dp"),
        P(),
    )
    return jax.shard_map(
        body,
        mesh=mesh,
        in_specs=placed,
        out_specs=(
            P(None, "hidden", "dp"),
            P("dp", "hidden"),
            P("dp", "hidden"),
            P("hidden", "dp"),
        ),
        check_vma=False,
    )
```

profile of v0, /device:TPU:1, one launch (start us, length us, event | category | flops | bytes accessed | tf_op | source)
XLA Modules:
  0.0 713.5 jit_solution(17066920279730390250)
XLA Ops:
  7.2 0.0 copy-start
  7.2 0.0 all-reduce.6.cloned.1.call-start
  7.2 37.5 %all_gather.16 = bf16[4,128,512]{2,1,0:T(8,128)(2,1)S(1)} all-gather(bf16[4,8,512]{2,1,0:T(8,128)(2,1)} %param.8), channel_id=1, replica_groups=mesh['dp'=16,'hidden'=16] {'hidden'}, dimensions={1}, use_global_device_ids=true | all-gather | bytes 557056 | tf_op jit(solution)/shard_map/all_gather | solution.py:46
  44.7 4.5 fusion.6
  49.2 3.6 reshape.163
  52.8 0.0 copy-done
  52.8 3.0 fusion.7
  55.8 0.0 copy-start.6
  55.8 3.7 reshape.164
  59.5 0.0 copy-done.6
  59.5 29.3 %all_gather.15 = bf16[4,128,512]{2,1,0:T(8,128)(2,1)S(1)} all-gather(bf16[4,8,512]{2,1,0:T(8,128)(2,1)S(1)} %copy-done.6), channel_id=1, replica_groups=mesh['dp'=16,'hidden'=16] {'hidden'}, dimensions={1}, use_global_device_ids=true | all-gather | bytes 557056 | tf_op jit(solution)/shard_map/all_gather | solution.py:47
  88.8 4.6 fusion.5
  93.4 3.7 reshape.161
  97.1 0.0 copy-start.7
  97.1 0.0 copy-start.8
  97.1 0.0 all-reduce.6.cloned.1.call-update
  97.1 0.0 all-gather.7.cloned.1.call-start
  97.2 0.5 copy-done.7
  97.7 0.6 fusion.4
  98.3 2.6 compare_select_fusion.1
  100.9 0.1 shift-left_multiply_fusion
  101.0 0.1 compare_bitcast_fusion
  101.1 0.2 copy.16
  101.3 0.0 copy-done.8
  101.4 0.6 dynamic-slice.6
  101.9 254.5 %all-reduce.6.cloned.1.call-done = (f32[16,57344]{1,0:T(8,128)}, f32[16,57344]{1,0:T(8,128)}, f32[16,57344]{1,0:T(8,128)}) async-done(((f32[16,57344]{1,0:T(8,128)}, f32[16,57344]{1,0:T(8,128)}, f32[16,57344]{1,0:T(8,128)}), (f32[16,57344]{1,0:T(8,128)}, f32[16,57344]{1,0:T(8,128)}, f32[16,57344]{1,0:T(8,128)})) %all-reduce.6.cloned.1.call-update) | async-done | bytes 11010064
  356.4 4.2 convert_bitcast_fusion
  360.6 5.2 convert_bitcast_fusion.1
  365.8 0.0 all-gather.7.cloned.1.call-update
  365.9 0.0 all-gather.9.cloned.1.call-start
  365.9 0.7 all-gather.9.cloned.1.call-update
  366.6 0.0 all-gather.11.cloned.1.call-start
  366.6 0.5 all-gather.11.cloned.1.call-update
  367.2 0.0 reduce-scatter.2.cloned.1.call-start
  367.2 73.5 %all-gather.7.cloned.1.call-done = bf16[16,1,57344]{2,1,0:T(2,128)(2,1)} async-done(((bf16[1,1,57344]{2,1,0:T(2,128)(2,1)}), bf16[16,1,57344]{2,1,0:T(2,128)(2,1)}) %all-gather.7.cloned.1.call-update) | async-done | bytes 1835024 | tf_op jit(solution)/shard_map/all_gather | solution.py:109
  440.7 13.1 %reduce.2 = bf16[16,57344]{1,0:T(8,128)(2,1)} reduce(bf16[16,1,57344]{2,1,0:T(2,128)(2,1)} %all-gather.7.cloned.1.call-done, bf16[]{:T(256)} %constant.117), dimensions={1}, to_apply=%all-gather.reduce_sub_computation | reduce | bytes 3670018 | tf_op jit(solution)/shard_map/all_gather | solution.py:109
  453.9 2.9 reshape.165
  456.8 71.9 %all-gather.9.cloned.1.call-done = bf16[16,1,57344]{2,1,0:T(2,128)(2,1)} async-done(((bf16[1,1,57344]{2,1,0:T(2,128)(2,1)}), bf16[16,1,57344]{2,1,0:T(2,128)(2,1)}) %all-gather.9.cloned.1.call-update) | async-done | bytes 1835024 | tf_op jit(solution)/shard_map/all_gather | solution.py:110
  528.7 13.0 %reduce.3 = bf16[16,57344]{1,0:T(8,128)(2,1)} reduce(bf16[16,1,57344]{2,1,0:T(2,128)(2,1)} %all-gather.9.cloned.1.call-done, bf16[]{:T(256)} %constant.117), dimensions={1}, to_apply=%all-gather.1.reduce_sub_computation | reduce | bytes 3670018 | tf_op jit(solution)/shard_map/all_gather | solution.py:110
  541.7 3.0 reshape.166
  544.7 0.0 copy-start.3
  544.7 0.0 copy-start.5
  544.7 2.8 fusion.8
  547.5 0.0 copy-done.3
  547.5 0.0 copy-done.5
  547.5 0.0 copy-start.2
  547.5 2.1 convolution_add_fusion
  549.7 0.0 reduce-scatter.2.cloned.1.call-update
  549.7 0.0 copy-done.2
  549.7 2.4 fusion
  552.1 0.0 copy-start.4
  552.1 3.9 copy.14
  556.0 0.0 copy-done.4
  556.0 2.4 fusion.1
  558.4 3.8 copy.15
  562.2 53.8 %all-gather.11.cloned.1.call-done = bf16[16,1,57344]{2,1,0:T(2,128)(2,1)} async-done(((bf16[1,1,57344]{2,1,0:T(2,128)(2,1)}), bf16[16,1,57344]{2,1,0:T(2,128)(2,1)}) %all-gather.11.cloned.1.call-update) | async-done | bytes 1835024 | tf_op jit(solution)/shard_map/all_gather | solution.py:108
  615.9 11.7 %reduce.4 = bf16[16,57344]{1,0:T(8,128)(2,1)S(1)} reduce(bf16[16,1,57344]{2,1,0:T(2,128)(2,1)} %all-gather.11.cloned.1.call-done, bf16[]{:T(256)} %constant.117), dimensions={1}, to_apply=%all-gather.2.reduce_sub_computation | reduce | bytes 3670018 | tf_op jit(solution)/shard_map/all_gather | solution.py:108
  627.7 1.9 reshape.168
  629.6 0.0 copy-start.1
  629.6 4.0 convolution_convert_fusion
  633.6 71.9 %reduce-scatter.2.cloned.1.call-done = f32[4,8,512]{2,1,0:T(8,128)} async-done(((f32[4,128,512]{2,1,0:T(8,128)}), f32[4,8,512]{2,1,0:T(8,128)}) %reduce-scatter.2.cloned.1.call-update) | async-done | bytes 65552 | tf_op jit(solution)/shard_map/reduce_scatter | solution.py:135
  705.5 1.5 convert_element_type.32
  706.9 0.0 copy-done.1
  (4 shorter events, 0.0 us)
Async XLA Ops:
  7.2 45.7 %copy-start = (bf16[512,1792]{1,0:T(8,128)(2,1)S(1)}, bf16[512,1792]{1,0:T(8,128)(2,1)}, u32[]{:S(2)}) copy-start(bf16[512,1792]{1,0:T(8,128)(2,1)} %param.10) | copy-start | bytes 5505028
  7.2 349.2 %all-reduce.6.cloned.1.call-start = ((), (), s32[]{:S(2)}) async-start(), calls=%async_computation.5 | async-start | bytes 22020096
  55.8 3.7 copy-start.6
  97.1 0.7 copy-start.7
  97.1 4.3 copy-start.8
  97.1 343.6 %all-gather.7.cloned.1.call-start = ((), (), s32[]{:S(2)}) async-start(), calls=%async_computation.2 | async-start | bytes 3899392 | tf_op jit(solution)/shard_map/all_gather | solution.py:109
  365.9 162.9 %all-gather.9.cloned.1.call-start = ((), (), s32[]{:S(2)}) async-start(), calls=%async_computation.3 | async-start | bytes 3899392 | tf_op jit(solution)/shard_map/all_gather | solution.py:110
  366.6 249.4 %all-gather.11.cloned.1.call-start = ((), (), s32[]{:S(2)}) async-start(), calls=%async_computation.4 | async-start | bytes 3899392 | tf_op jit(solution)/shard_map/all_gather | solution.py:108
  367.2 338.3 %reduce-scatter.2.cloned.1.call-start = ((), (), s32[]{:S(2)}) async-start(), calls=%async_computation.1 | async-start | bytes 1114112 | tf_op jit(solution)/shard_map/reduce_scatter | solution.py:135
  544.7 2.8 copy-start.3
  544.7 2.8 copy-start.5
  547.5 2.2 copy-start.2
  552.1 3.9 copy-start.4
  629.6 77.4 %copy-start.1 = (bf16[512,1792]{1,0:T(8,128)(2,1)S(1)}, bf16[512,1792]{1,0:T(8,128)(2,1)}, u32[]{:S(2)}) copy-start(bf16[512,1792]{1,0:T(8,128)(2,1)} %param.10) | copy-start | bytes 5505028
Sparse Core Ops, SparseCore 0:
  97.2 259.1 all-reduce.5
  366.0 74.7 all-gather.6
  443.1 85.5 all-gather.8
  530.4 85.5 all-gather.10
  619.9 85.5 reduce-scatter.1
where the time goes:
time: 715 us; the launch traced here: 713 us
  waiting for transfers between devices  527 us (74%)
  blocking collectives  66.8 us (9%)
  other arithmetic  51.5 us (7%)
  local copies, waits for them, and re-layouts  28.5 us (4%)
  matrix products  25.7 us (4%)
  between operations  13.9 us (2%)
    unnamed x6, waiting for transfers between devices  256 us
    all_gather x1, waiting for transfers between devices, body(): lax.all_gather(dgate_pack, 'dp', axis=0, tiled=True)  73.5 us
    all_gather x1, waiting for transfers between devices, body(): lax.all_gather(dup_pack, 'dp', axis=0, tiled=True)  71.9 us
    reduce_scatter x1, waiting for transfers between devices, body(): lax.psum_scatter(input_sum, 'hidden', scatter_dimension=1, tiled=True)  71.9 us
    all_gather x1, waiting for transfers between devices, body(): lax.all_gather(act_pack, 'dp', axis=0, tiled=True)  53.8 us
    all_gather x1, blocking collectives, body(): lax.all_gather(activations, 'hidden', axis=1, tiled=True)  37.5 us
    all_gather x1, blocking collectives, body(): lax.all_gather(out_grad, 'hidden', axis=1, tiled=True)  29.3 us
  transfers between devices with their start and end apart: 5, of which 5 were waited for; matrix products, arithmetic and copies ran while one was open for 10% of the time, Pallas kernels for 0%

commit v1 on v0

v1 whole, which is shorter than its diff:
```python
import functools

import jax
import jax.numpy as jnp
from jax import lax
from jax.experimental import pallas as pl
from jax.experimental.pallas import tpu as pltpu
from jax.sharding import PartitionSpec as P

MESH = pl.DeviceIdType.MESH
BF16 = jnp.bfloat16
F32 = jnp.float32

UNITS = 4
TOK = 128
FEAT = 512
WIDTH = 1792
HALF = WIDTH // 2
TILE = 256
CHIPS = 8
NT = (((1,), (1,)), ((), ()))


def device(z, y, chip, core):
    return (z * 4 + y, chip * 2 + core)


def active_count(chip):
    return 1 + (chip < 4).astype(jnp.int32) + (chip < 2) + (chip < 1)


def kernel(
    lev, x_ref, g_ref, wg_hbm, wu_hbm, wd_hbm,
    in_grad, x_out, g_out, act_hbm, dg_hbm, du_hbm,
    wg, wu, wd, own, pair, xg, pf, pb, r1, r2, zr, agb, term, pair_t, hr, fs, fr,
    w_sem, o_sem, a_send, a_recv, s_send, s_recv, h_send, h_recv,
):
    dp = lax.axis_index("dp")
    hidden = lax.axis_index("hidden")
    z, y = dp // 4, dp % 4
    chip, core = hidden // 2, hidden % 2
    xx, zh = chip // 2, chip % 2
    other = 1 - core
    n = active_count(chip)
    y_opp, y_right, y_left = (y + 2) % 4, (y + 1) % 4, (y + 3) % 4
    partner = device(z, y, chip, other)
    right, left = device(z, y_right, chip, core), device(z, y_left, chip, core)

    def remote(src, dst, send, recv, target):
        return pltpu.make_async_remote_copy(
            src_ref=src, dst_ref=dst, send_sem=send, recv_sem=recv, device_id=target, device_id_type=MESH
        )

    loads = [
        pltpu.make_async_copy(src, dst, w_sem.at[k])
        for k, (src, dst) in enumerate(((wg_hbm, wg), (wu_hbm, wu), (wd_hbm, wd)))
    ]
    for load in loads:
        load.start()

    barrier = pltpu.get_barrier_semaphore()
    greeted = [partner, right, left]
    greeted += [device((z + k) % 4, y, chip, core) for k in (1, 2, 3)]
    greeted += [device(z, y, (chip + k) % CHIPS, core) for k in range(1, CHIPS)]
    for who in greeted:
        pl.semaphore_signal(barrier, inc=1, device_id=who, device_id_type=MESH)

    for array, ref in enumerate((x_ref, g_ref)):
        rows = []
        for u in range(UNITS):
            index = jnp.int32(0)
            for i in range(1, UNITS):
                index = jnp.where(lev[i] == UNITS - 1 - u, i, index)
            rows.append(ref[index].astype(F32))
        own[array * 32 : array * 32 + 16] = jnp.concatenate(rows[:2], 0).astype(BF16)
        own[array * 32 + 16 : array * 32 + 32] = jnp.concatenate(rows[2:], 0).astype(BF16)

    pl.semaphore_wait(barrier, len(greeted))

    pair_copy = remote(own, pair, a_send.at[0], a_recv.at[0], partner)
    pair_copy.start()
    pair_copy.wait()
    for u in range(0, UNITS, 2):
        rows = pl.ds(pl.multiple_of(core * 32 + u * 8, 16), 16)
        mine, theirs = own[rows].astype(F32), pair[rows].astype(F32)
        zero = jnp.where(core == 0, mine, theirs)
        one = jnp.where(core == 0, theirs, mine)
        xg[core, u, chip] = jnp.concatenate([zero[:8], one[:8]], 0).astype(BF16)
        xg[core, u + 1, chip] = jnp.concatenate([zero[8:], one[8:]], 0).astype(BF16)

    def block(c):
        return xg.at[core, :, c]

    far = 2 * xx + (1 - zh)
    spread = [remote(block(chip), block(chip), a_send.at[1], a_recv.at[1], device(z, y, far, core))]
    for k in (1, 2, 3):
        target = device(z, y, 2 * ((xx + k) % 4) + zh, core)
        spread.append(remote(block(chip), block(chip), a_send.at[1 + k], a_recv.at[1 + k], target))
    for copy in spread:
        copy.start()
    spread[0].wait_recv()
    for k in (1, 2, 3):
        target = device(z, y, 2 * ((xx + k) % 4) + zh, core)
        spread.append(remote(block(far), block(far), a_send.at[4 + k], a_recv.at[4 + k], target))
        spread[-1].start()
    for copy in spread[1:]:
        copy.wait_recv()
    for copy in spread:
        copy.wait_send()
    swap = remote(xg.at[core], xg.at[core], a_send.at[8], a_recv.at[8], partner)
    swap.start()
    swap.wait()
    for load in loads:
        load.wait()

    def own_piece(ref, u):
        return ref.at[u, :, pl.ds(y * 32 + (z // 2) * 16, 16), pl.ds(pl.multiple_of((z % 2) * HALF, HALF), HALF)]

    def part(ref, u, yy, half, count=16):
        return ref.at[u, :, pl.ds(yy * 32 + half * 16, count), :]

    def copy_of(u, kind):
        if kind == 0:
            src, dst, to = part(pb, u, y_opp, 0), r1.at[u, 0], right
        elif kind == 1:
            src, dst, to = part(pb, u, y_opp, 1), r1.at[u, 1], left
        elif kind == 2:
            src, dst, to = part(pb, u, y_right, 1), r2.at[u, 0, :, pl.ds(16, 16), :], right
        elif kind == 3:
            src, dst, to = part(pb, u, y_left, 0), r2.at[u, 1, :, pl.ds(0, 16), :], left
        elif kind == 4:
            src, dst, to = r1.at[u, 0], r2.at[u, 0, :, pl.ds(0, 16), :], right
        elif kind == 5:
            src, dst, to = r1.at[u, 1], r2.at[u, 1, :, pl.ds(16, 16), :], left
        elif kind in (6, 7, 8):
            zd = (z + kind - 5) % 4
            src = pf.at[
                u, :, pl.ds(y * 32 + (zd // 2) * 16, 16), pl.ds(pl.multiple_of((zd % 2) * HALF, HALF), HALF)
            ]
            dst, to = zr.at[u, kind - 6], device(zd, y, chip, core)
        elif kind in (9, 10, 11):
            src = dst = own_piece(agb, u)
            to = device((z + kind - 8) % 4, y, chip, core)
        elif kind == 12:
            src, to = part(agb, u, y, 0, 32), right
            dst = src
        elif kind == 13:
            src, to = part(agb, u, y, 0, 32), left
            dst = src
        elif kind == 14:
            src, to = part(agb, u, y_left, 0), right
            dst = src
        else:
            src, to = part(agb, u, y_right, 1), left
            dst = src
        return remote(src, dst, s_send.at[u, kind], s_recv.at[u, kind], to)

    def pair_term(u):
        return remote(term.at[u, other], pair_t.at[u], h_send.at[u, 7], h_recv.at[u, 8], partner)

    def chip_term(u, k):
        target = (chip + k) % CHIPS
        return remote(
            term.at[u, core, pl.ds(target * 16, 16), :], hr.at[u, chip],
            h_send.at[u, k - 1], h_recv.at[u, chip], device(z, y, target, core),
        )

    def dots(u):
        def tile(i, _):
            cols = pl.ds(pl.multiple_of(i * TILE, TILE), TILE)
            rows_x = xg[0, u].reshape(TOK, FEAT)
            rows_g = xg[1, u].reshape(TOK, FEAT)
            values = (
                jnp.dot(rows_x, wg[:, cols], preferred_element_type=F32),
                jnp.dot(rows_x, wu[:, cols], preferred_element_type=F32),
                lax.dot_general(rows_g, wd[cols, :], NT, preferred_element_type=F32),
            )
            for k, value in enumerate(values):
                pf[u, k, :, cols] = value
                pb[u, k, :, cols] = value.astype(BF16)
            return 0

        lax.fori_loop(0, WIDTH // TILE, tile, 0)
        for kind in range(4):
            copy_of(u, kind).start()

    def accumulate(u):
        for side, (kind, yy) in enumerate(((0, y_right), (1, y_left))):
            copy_of(u, kind).wait_recv()
            rows = pl.ds(yy * 32 + side * 16, 16)
            for k in range(3):
                r1[u, side, k] = (r1[u, side, k].astype(F32) + pf[u, k, rows, :]).astype(BF16)
            copy_of(u, kind + 4).start()

    def sum_y(u):
        for kind in (2, 3, 4, 5):
            copy_of(u, kind).wait_recv()
        rows = pl.ds(y * 32, 32)
        for k in range(3):
            pf[u, k, rows, :] += r2[u, 0, k].astype(F32) + r2[u, 1, k].astype(F32)
        for kind in (6, 7, 8):
            copy_of(u, kind).start()

    def units(u):
        for kind in (6, 7, 8):
            copy_of(u, kind).wait_recv()
        rows = pl.ds(y * 32 + (z // 2) * 16, 16)
        cols = pl.ds(pl.multiple_of((z % 2) * HALF, HALF), HALF)
        gate, up, grad = (
            pf[u, k, rows, cols] + (zr[u, 0, k] + zr[u, 1, k] + zr[u, 2, k]) for k in range(3)
        )
        s = jax.nn.sigmoid(gate)
        agb[u, 0, rows, cols] = (gate * s * up).astype(BF16)
        agb[u, 1, rows, cols] = (grad * up * s * (1.0 + gate * (1.0 - s))).astype(BF16)
        agb[u, 2, rows, cols] = (grad * gate * s).astype(BF16)
        for kind in (9, 10, 11):
            copy_of(u, kind).start()

    def spread_y(u):
        for kind in (9, 10, 11):
            copy_of(u, kind).wait_recv()
        for kind in (12, 13):
            copy_of(u, kind).start()

    def forward_y(u):
        for kind in (12, 13):
            copy_of(u, kind).wait_recv()
            copy_of(u, kind + 2).start()

    def save(u, k):
        out = (act_hbm, dg_hbm, du_hbm)[k]
        return pltpu.make_async_copy(agb.at[u, k], out.at[pl.ds(u * TOK, TOK), :], o_sem.at[u, k])

    def back(u):
        for kind in (14, 15):
            copy_of(u, kind).wait_recv()
        for half in range(2):
            feats = slice(half * TILE, half * TILE + TILE)
            term[u, half] = lax.dot_general(
                agb[u, 1], wg[feats, :], NT, preferred_element_type=F32
            ) + lax.dot_general(agb[u, 2], wu[feats, :], NT, preferred_element_type=F32)
        pair_term(u).start()
        for k in range(3):
            save(u, k).start()

    def send_terms(u):
        pair_term(u).wait_recv()
        term[u, core] += pair_t[u]
        for k in range(1, CHIPS):
            chip_term(u, k).start()

    stages = (dots, accumulate, sum_y, units, spread_y, forward_y, back, send_terms)

    def step(t, _):
        for lag in reversed(range(len(stages))):
            u = t - lag

            @pl.when(jnp.logical_and(u >= 0, u < n))
            def _(u=u, lag=lag):
                stages[lag](u)

        return 0

    lax.fori_loop(0, n + len(stages) - 1, step, 0)

    def clear(u, _):
        agb[u] = jnp.zeros((3, TOK, WIDTH), BF16)
        for k in range(3):
            save(u, k).start()
        return 0

    lax.fori_loop(n, UNITS, clear, 0)

    for u in range(UNITS):
        fs[u] = jnp.zeros((16, TILE), F32)

        def add(j, _, u=u):
            @pl.when(j == chip)
            def _():
                fs[u] += term[u, core, pl.ds(chip * 16, 16), :]

            @pl.when(j != chip)
            def _():
                remote(
                    hr.at[u, j], hr.at[u, j], h_send.at[u, 0], h_recv.at[u, j], device(z, y, j, core)
                ).wait_recv()
                fs[u] += hr[u, j]

            return 0

        lax.fori_loop(0, (8, 4, 2, 1)[u], add, 0)

    last = remote(
        fs.at[:, pl.ds(pl.multiple_of(other * 8, 8), 8), :], fr, a_send.at[9], a_recv.at[9], partner
    )
    last.start()
    last.wait()
    here = pl.ds(pl.multiple_of(core * TILE, TILE), TILE)
    there = pl.ds(pl.multiple_of(other * TILE, TILE), TILE)
    mine = pl.ds(pl.multiple_of(core * 8, 8), 8)
    for b in range(UNITS):
        u = UNITS - 1 - lev[b]
        in_grad[b, :, here] = fs[u, mine, :].astype(BF16)
        in_grad[b, :, there] = fr[u].astype(BF16)
    x_out[...] = xg[0].reshape(UNITS * TOK, FEAT)
    g_out[...] = xg[1].reshape(UNITS * TOK, FEAT)

    def drain(u, _):
        for kind in range(16):
            copy_of(u, kind).wait_send()
        pair_term(u).wait_send()
        for k in range(1, CHIPS):
            chip_term(u, k).wait_send()
        return 0

    lax.fori_loop(0, n, drain, 0)
    for u in range(UNITS):
        for k in range(3):
            save(u, k).wait()


def exchange(levels, activations, out_grad, w_gate, w_up, w_down):
    rows = UNITS * TOK
    vmem = pl.BlockSpec(memory_space=pltpu.VMEM)
    hbm = pl.BlockSpec(memory_space=pl.ANY)
    dma = pltpu.SemaphoreType.DMA
    return pl.pallas_call(
        kernel,
        out_shape=[
            jax.ShapeDtypeStruct(activations.shape, BF16),
            jax.ShapeDtypeStruct((rows, FEAT), BF16),
            jax.ShapeDtypeStruct((rows, FEAT), BF16),
            jax.ShapeDtypeStruct((rows, WIDTH), BF16),
            jax.ShapeDtypeStruct((rows, WIDTH), BF16),
            jax.ShapeDtypeStruct((rows, WIDTH), BF16),
        ],
        in_specs=[pl.BlockSpec(memory_space=pltpu.SMEM), vmem, vmem, hbm, hbm, hbm],
        out_specs=[vmem, vmem, vmem, hbm, hbm, hbm],
        scratch_shapes=[
            pltpu.VMEM((FEAT, WIDTH), BF16),
            pltpu.VMEM((FEAT, WIDTH), BF16),
            pltpu.VMEM((WIDTH, FEAT), BF16),
            pltpu.VMEM((64, FEAT), BF16),
            pltpu.VMEM((64, FEAT), BF16),
            pltpu.VMEM((2, UNITS, CHIPS, 16, FEAT), BF16),
            pltpu.VMEM((UNITS, 3, TOK, WIDTH), F32),
            pltpu.VMEM((UNITS, 3, TOK, WIDTH), BF16),
            pltpu.VMEM((UNITS, 2, 3, 16, WIDTH), BF16),
            pltpu.VMEM((UNITS, 2, 3, 32, WIDTH), BF16),
            pltpu.VMEM((UNITS, 3, 3, 16, HALF), F32),
            pltpu.VMEM((UNITS, 3, TOK, WIDTH), BF16),
            pltpu.VMEM((UNITS, 2, TOK, TILE), F32),
            pltpu.VMEM((UNITS, TOK, TILE), F32),
            pltpu.VMEM((UNITS, CHIPS, 16, TILE), F32),
            pltpu.VMEM((UNITS, 16, TILE), F32),
            pltpu.VMEM((UNITS, 8, TILE), F32),
            dma((3,)),
            dma((UNITS, 3)),
            dma((10,)),
            dma((10,)),
            dma((UNITS, 16)),
            dma((UNITS, 16)),
            dma((UNITS, 8)),
            dma((UNITS, 9)),
        ],
        compiler_params=pltpu.CompilerParams(
            collective_id=0, has_side_effects=True, vmem_limit_bytes=56 * 1024 * 1024
        ),
    )(levels, activations, out_grad, w_gate, w_up, w_down)


def body(activations, out_grad, w_gate, w_up, w_down, levels):
    input_grad, rows_x, rows_g, act, dgate, dup = exchange(
        levels, activations, out_grad, w_gate, w_up, w_down
    )
    contract_rows = (((0,), (0,)), ((), ()))
    dot = functools.partial(
        lax.dot_general, dimension_numbers=contract_rows, preferred_element_type=F32
    )
    return (
        input_grad,
        dot(rows_x, dgate).astype(BF16),
        dot(rows_x, dup).astype(BF16),
        dot(act, rows_g).astype(BF16),
    )


def solution(mesh):
    placed = (
        P(None, "hidden", "dp"),
        P(None, "hidden", "dp"),
        P("dp", "hidden"),
        P("dp", "hidden"),
        P("hidden", "dp"),
        P(),
    )
    return jax.shard_map(
        body,
        mesh=mesh,
        in_specs=placed,
        out_specs=(
            P(None, "hidden", "dp"),
            P("dp", "hidden"),
            P("dp", "hidden"),
            P("hidden", "dp"),
        ),
        check_vma=False,
    )
```

time: 715 us -> 175 us (0.24)
  waiting for transfers between devices: 527 us -> 0 us
  Pallas kernels: 0 us -> 163 us
  blocking collectives: 66.8 us -> 0 us
  other arithmetic: 51.5 us -> 0 us
  local copies, waits for them, and re-layouts: 28.5 us -> 0.63 us
  matrix products: 25.7 us -> 8.94 us
  between operations: 13.9 us -> 0.67 us
    unnamed x6 -> x0, waiting for transfers between devices: 256 us -> none
    all_gather x3 -> x0, waiting for transfers between devices: 199 us -> none  [the longest x1 73.5 us: body(): lax.all_gather(dgate_pack, 'dp', axis=0, tiled=True)]
    pallas_call x0 -> x1, Pallas kernels: none -> 163 us  [exchange(): pl.pallas_call(kernel, out_shape=[jax.ShapeDtypeStruct(activations.shape,...]
    reduce_scatter x1 -> x0, waiting for transfers between devices: 71.9 us -> none  [body(): lax.psum_scatter(input_sum, 'hidden', scatter_dimension=1, tiled=True)]
    all_gather x2 -> x0, blocking collectives: 66.8 us -> none  [the longest x1 37.5 us: body(): lax.all_gather(activations, 'hidden', axis=1, tiled=True)]
    all_gather x3 -> x0, other arithmetic: 37.8 us -> none  [the longest x1 13.1 us: body(): lax.all_gather(dgate_pack, 'dp', axis=0, tiled=True)]
    reshape x6 -> x0, local copies, waits for them, and re-layouts: 18.8 us -> none  [the longest x3 11 us: flatten_parts(): part.reshape(leading, -1)]
    dot_general x8 -> x3, matrix products: 25.7 us -> 8.94 us  [the longest x1 4.18 us: body(): dot(rows_x, dgate).astype(BF16)]
  transfers between devices with their start and end apart: 5 -> 0, of which waited for: 5 -> 0; matrix products, arithmetic and copies ran while one was open for 10% -> 0% of each run, Pallas kernels for 0% -> 0%
where the time goes in v1:
time: 175 us; the launch traced here: 173 us
  Pallas kernels  163 us (93%)
  matrix products  8.94 us (5%)
    pallas_call x1, Pallas kernels, exchange(): pl.pallas_call(kernel, out_shape=[jax.ShapeDtypeStruct(activations.shape,...  163 us
    dot_general x1, matrix products, body(): dot(rows_x, dgate).astype(BF16)  4.18 us

profile of v1, /device:TPU:1, one launch (start us, length us, event | category | flops | bytes accessed | tf_op | source)
XLA Modules:
  0.0 172.8 jit_solution(7138129420225516261)
XLA Ops:
  0.6 162.5 %shard_map.93 = (bf16[4,8,512]{2,1,0:T(8,128)(2,1)}, bf16[512,512]{1,0:T(8,128)(2,1)}, bf16[512,512]{1,0:T(8,128)(2,1)}, bf16[512,1792]{1,0:T(8,128)(2,1)}, bf16...) custom-call(s32[4]{0:T(128)} %lev.1, bf16[4,8,512]{2,1,0:T(8,128)(2,1)} %x_ref.1, bf16[4,8,512]{2,1,0:T(8,128)(2,1)} %g_ref.1, ...), custom_call_target="tpu_custom_call" | custom-call | tf_op jit(solution)/shard_map/pallas_call | solution.py:327
  163.2 0.0 copy-start.2
  163.2 0.0 copy-start.4
  163.2 4.2 %convolution_convert_fusion.2 = bf16[512,1792]{1,0:T(8,128)(2,1)} fusion(bf16[512,512]{1,0:T(8,128)(2,1)} %get-tuple-element.11, bf16[512,1792]{1,0:T(8,128)(2,1)} %get-tuple-element.12), kind=kOutput, calls=%fused_computation.2 | convolution fusion | flops 940441600 | bytes 4194304 | tf_op jit(solution)/shard_map/dot_general | solution.py:382
  167.4 0.0 copy-done.2
  167.4 0.0 copy-done.4
  167.4 0.0 copy-start.1
  167.4 0.0 copy-start.3
  167.4 2.4 %convolution_convert_fusion.1 = bf16[512,1792]{1,0:T(8,128)(2,1)} fusion(bf16[512,512]{1,0:T(8,128)(2,1)S(1)} %copy-done.4, bf16[512,1792]{1,0:T(8,128)(2,1)S(1)} %copy-done.2), kind=kOutput, calls=%fused_computation.1 | convolution fusion | flops 940441600 | bytes 4194304 | tf_op jit(solution)/shard_map/dot_general | solution.py:383
  169.8 0.0 copy-done.1
  169.8 0.0 copy-done.3
  169.8 0.0 copy-start
  169.8 2.4 %convolution_convert_fusion = bf16[1792,512]{1,0:T(8,128)(2,1)} fusion(bf16[512,1792]{1,0:T(8,128)(2,1)S(1)} %copy-done.1, bf16[512,512]{1,0:T(8,128)(2,1)S(1)} %copy-done.3), kind=kOutput, calls=%fused_computation | convolution fusion | flops 940441600 | bytes 4194304 | tf_op jit(solution)/shard_map/dot_general | solution.py:384
  172.2 0.0 copy-done
  172.2 0.6 copy.11
Async XLA Ops:
  163.2 4.2 %copy-start.2 = (bf16[512,1792]{1,0:T(8,128)(2,1)S(1)}, bf16[512,1792]{1,0:T(8,128)(2,1)}, u32[]{:S(2)}) copy-start(bf16[512,1792]{1,0:T(8,128)(2,1)} %get-tuple-element.13) | copy-start | bytes 5505028
  163.2 4.2 %copy-start.4 = (bf16[512,512]{1,0:T(8,128)(2,1)S(1)}, bf16[512,512]{1,0:T(8,128)(2,1)}, u32[]{:S(2)}) copy-start(bf16[512,512]{1,0:T(8,128)(2,1)} %get-tuple-element.11) | copy-start | bytes 1572868
  167.4 2.4 %copy-start.1 = (bf16[512,1792]{1,0:T(8,128)(2,1)S(1)}, bf16[512,1792]{1,0:T(8,128)(2,1)}, u32[]{:S(2)}) copy-start(bf16[512,1792]{1,0:T(8,128)(2,1)} %get-tuple-element.14) | copy-start | bytes 5505028
  167.4 2.4 %copy-start.3 = (bf16[512,512]{1,0:T(8,128)(2,1)S(1)}, bf16[512,512]{1,0:T(8,128)(2,1)}, u32[]{:S(2)}) copy-start(bf16[512,512]{1,0:T(8,128)(2,1)} %get-tuple-element.15) | copy-start | bytes 1572868
  169.8 2.4 %copy-start = (bf16[4,8,512]{2,1,0:T(8,128)(2,1)S(1)}, bf16[4,8,512]{2,1,0:T(8,128)(2,1)}, u32[]{:S(2)}) copy-start(bf16[4,8,512]{2,1,0:T(8,128)(2,1)} %get-tuple-element.20) | copy-start | bytes 98308

commit v2 on v1

v2 whole, which is shorter than its diff:
```python
import jax
import jax.numpy as jnp
from jax import lax
from jax.experimental import pallas as pl
from jax.experimental.pallas import tpu as pltpu
from jax.sharding import PartitionSpec as P

MESH = pl.DeviceIdType.MESH
BF16 = jnp.bfloat16
F32 = jnp.float32

UNITS = 4
TOK = 128
FEAT = 512
WIDTH = 1792
TILE = 256
CHIPS = 8
SPANS = ((0, 512), (512, 512), (1024, 768))
LENT = {(3, 0): 1, (3, 1): 3, (3, 2): 2}
NT = (((1,), (1,)), ((), ()))
ORDER_LENDER = (3, 2, 1, 0)
ORDER = (0, 3, 1, 2)
LAGS = (0, 2, 4, 6, 8, 10, 12, 14)


def device(z, y, chip, core):
    return (z * 4 + y, chip * 2 + core)


def active_count(chip):
    return 1 + (chip < 4).astype(jnp.int32) + (chip < 2) + (chip < 1)


def kernel(
    lev, x_ref, g_ref, wg_hbm, wu_hbm, wd_hbm,
    in_grad, gate_hbm, up_hbm, down_hbm,
    wg, wu, wd, own, pair, xg, pf, pb, r1, r2, zr, zs, zx, agb, term, pair_t, hr, fs, fr, xt, gate_v, up_v, down_v,
    w_sem, o_sem, a_send, a_recv, s_send, s_recv, h_send, h_recv,
):
    dp = lax.axis_index("dp")
    hidden = lax.axis_index("hidden")
    z, y = dp // 4, dp % 4
    chip, core = hidden // 2, hidden % 2
    xx, zh = chip // 2, chip % 2
    other = 1 - core
    n = active_count(chip)
    z_pair = z + 1 - 2 * (z % 2)
    inner = jnp.logical_or(z == 1, z == 2)
    outer = jnp.logical_not(inner)
    y_opp, y_right, y_left = (y + 2) % 4, (y + 1) % 4, (y + 3) % 4
    partner = device(z, y, chip, other)
    right, left = device(z, y_right, chip, core), device(z, y_left, chip, core)

    def remote(src, dst, send, recv, target):
        return pltpu.make_async_remote_copy(
            src_ref=src, dst_ref=dst, send_sem=send, recv_sem=recv, device_id=target, device_id_type=MESH
        )

    loads = [
        pltpu.make_async_copy(src, dst, w_sem.at[k])
        for k, (src, dst) in enumerate(((wg_hbm, wg), (wu_hbm, wu), (wd_hbm, wd)))
    ]
    for load in loads:
        load.start()

    barrier = pltpu.get_barrier_semaphore()
    greeted = [partner, right, left]
    greeted += [device((z + k) % 4, y, chip, core) for k in (1, 2, 3)]
    greeted += [device(z, y, (chip + k) % CHIPS, core) for k in range(1, CHIPS)]
    for who in greeted:
        pl.semaphore_signal(barrier, inc=1, device_id=who, device_id_type=MESH)

    for array, ref in enumerate((x_ref, g_ref)):
        rows = []
        for u in range(UNITS):
            index = jnp.int32(0)
            for i in range(1, UNITS):
                index = jnp.where(lev[i] == UNITS - 1 - u, i, index)
            rows.append(ref[index].astype(F32))
        own[array * 32 : array * 32 + 16] = jnp.concatenate(rows[:2], 0).astype(BF16)
        own[array * 32 + 16 : array * 32 + 32] = jnp.concatenate(rows[2:], 0).astype(BF16)

    pl.semaphore_wait(barrier, len(greeted))

    pair_copy = remote(own, pair, a_send.at[0], a_recv.at[0], partner)
    pair_copy.start()
    pair_copy.wait()
    for u in range(0, UNITS, 2):
        rows = pl.ds(pl.multiple_of(core * 32 + u * 8, 16), 16)
        mine, theirs = own[rows].astype(F32), pair[rows].astype(F32)
        zero = jnp.where(core == 0, mine, theirs)
        one = jnp.where(core == 0, theirs, mine)
        xg[core, u, chip] = jnp.concatenate([zero[:8], one[:8]], 0).astype(BF16)
        xg[core, u + 1, chip] = jnp.concatenate([zero[8:], one[8:]], 0).astype(BF16)

    def block(c):
        return xg.at[core, :, c]

    far = 2 * xx + (1 - zh)
    spread = [remote(block(chip), block(chip), a_send.at[1], a_recv.at[1], device(z, y, far, core))]
    for k in (1, 2, 3):
        target = device(z, y, 2 * ((xx + k) % 4) + zh, core)
        spread.append(remote(block(chip), block(chip), a_send.at[1 + k], a_recv.at[1 + k], target))
    for copy in spread:
        copy.start()
    spread[0].wait_recv()
    for k in (1, 2, 3):
        target = device(z, y, 2 * ((xx + k) % 4) + zh, core)
        spread.append(remote(block(far), block(far), a_send.at[4 + k], a_recv.at[4 + k], target))
        spread[-1].start()
    for copy in spread[1:]:
        copy.wait_recv()
    for copy in spread:
        copy.wait_send()
    swap = remote(xg.at[core], xg.at[core], a_send.at[8], a_recv.at[8], partner)
    swap.start()
    swap.wait()
    for load in loads:
        load.wait()

    def piece(zd, q):
        first, width = SPANS[q]
        cols = pl.ds(pl.multiple_of(first + (zd % 2) * (width // 2), 128), width // 2)
        return pl.ds(y * 32 + (zd // 2) * 16, 16), cols

    def copy_of(u, q, kind):
        span = pl.ds(*SPANS[q])
        half_span = pl.ds(SPANS[q][0] // 2, SPANS[q][1] // 2)

        def part(ref, u, yy, half, count=16):
            return ref.at[u, :, pl.ds(yy * 32 + half * 16, count), span]

        if kind == 0:
            src, dst, to = part(pb, u, y_opp, 0), r1.at[u, 0, :, :, span], right
        elif kind == 1:
            src, dst, to = part(pb, u, y_opp, 1), r1.at[u, 1, :, :, span], left
        elif kind == 2:
            src, dst, to = part(pb, u, y_right, 1), r2.at[u, 0, :, pl.ds(16, 16), span], right
        elif kind == 3:
            src, dst, to = part(pb, u, y_left, 0), r2.at[u, 1, :, pl.ds(0, 16), span], left
        elif kind == 4:
            src, dst, to = r1.at[u, 0, :, :, span], r2.at[u, 0, :, pl.ds(0, 16), span], right
        elif kind == 5:
            src, dst, to = r1.at[u, 1, :, :, span], r2.at[u, 1, :, pl.ds(16, 16), span], left
        elif kind == 6:
            rows, cols = piece(z_pair, q)
            src = pf.at[u, :, rows, cols]
            dst, to = zr.at[u, 0, :, :, half_span], device(z_pair, y, chip, core)
        elif kind == 7:
            src, dst, to = zs.at[u, :, :, span], zx.at[u, :, :, span], device(z_pair, y, chip, core)
        elif kind in (8, 9):
            zd = 2 * (1 - z // 2) + kind - 8
            rows, cols = piece(zd, q)
            src = pf.at[u, :, rows, cols]
            dst, to = zr.at[u, 1, :, :, half_span], device(zd, y, chip, core)
        elif kind in (10, 11, 12):
            rows, cols = piece(z, q)
            src = dst = agb.at[u, :, rows, cols]
            to = device((z + kind - 9) % 4, y, chip, core)
        elif kind in (13, 14):
            src = dst = part(agb, u, y, 0, 32)
            to = (right, left)[kind - 13]
        elif kind == 15:
            src = dst = part(agb, u, y_left, 0)
            to = right
        elif kind == 16:
            src = dst = part(agb, u, y_right, 1)
            to = left
        elif kind == 17:
            src = dst = pb.at[u, :, :, span]
            to = device(z, y, 2 * lender(u, q) + zh, core)
        else:
            src = dst = agb.at[u, :, :, span]
            to = device(z, y, zh, core)
        return remote(src, dst, s_send.at[u, q, kind], s_recv.at[u, q, 8 if kind == 9 else kind], to)

    def lender(u, q):
        where = jnp.int32(1)
        for (unit, span), x_to in LENT.items():
            if span == q:
                where = jnp.where(u == unit, x_to, where)
        return where

    def lent(u, q):
        found = jnp.bool_(False)
        for unit, span in LENT:
            if span == q:
                found = jnp.logical_or(found, u == unit)
        return jnp.logical_and(found, jnp.logical_and(xx == 0, u < n))

    def taken(u, q):
        found = jnp.bool_(False)
        for (unit, span), x_to in LENT.items():
            if span == q:
                found = jnp.logical_or(found, jnp.logical_and(u == unit, xx == x_to))
        return jnp.logical_and(found, u < active_count(zh))

    def pair_term(u):
        return remote(term.at[u, other], pair_t.at[u], h_send.at[u, 7], h_recv.at[u, 8], partner)

    def chip_term(u, k):
        target = (chip + k) % CHIPS
        return remote(
            term.at[u, core, pl.ds(target * 16, 16), :], hr.at[u, chip],
            h_send.at[u, k - 1], h_recv.at[u, chip], device(z, y, target, core),
        )

    def dots(u, q):
        def tile(i, _):
            cols = pl.ds(pl.multiple_of(i * TILE, TILE), TILE)
            rows_x = xg[0, u].reshape(TOK, FEAT)
            rows_g = xg[1, u].reshape(TOK, FEAT)
            values = (
                jnp.dot(rows_x, wg[:, cols], preferred_element_type=F32),
                jnp.dot(rows_x, wu[:, cols], preferred_element_type=F32),
                lax.dot_general(rows_g, wd[cols, :], NT, preferred_element_type=F32),
            )
            for k, value in enumerate(values):
                pf[u, k, :, cols] = value
                pb[u, k, :, cols] = value.astype(BF16)
            return 0

        first, width = SPANS[q]

        @pl.when(u < n)
        def _():
            lax.fori_loop(first // TILE, (first + width) // TILE, tile, 0)

        @pl.when(lent(u, q))
        def _():
            copy_of(u, q, 17).start()

        @pl.when(taken(u, q))
        def _():
            copy_of(u, q, 17).wait_recv()
            for k in range(3):
                pf[u, k, :, first : first + width] = pb[u, k, :, first : first + width].astype(F32)

        @pl.when(jnp.logical_not(lent(u, q)))
        def _():
            for kind in range(4):
                copy_of(u, q, kind).start()

    def accumulate(u, q):
        span = pl.ds(*SPANS[q])
        for side, (kind, yy) in enumerate(((0, y_right), (1, y_left))):
            copy_of(u, q, kind).wait_recv()
            rows = pl.ds(yy * 32 + side * 16, 16)
            for k in range(3):
                r1[u, side, k, :, span] = (r1[u, side, k, :, span].astype(F32) + pf[u, k, rows, span]).astype(BF16)
            copy_of(u, q, kind + 4).start()

    def sum_y(u, q):
        span = pl.ds(*SPANS[q])
        for kind in (2, 3, 4, 5):
            copy_of(u, q, kind).wait_recv()
        rows = pl.ds(y * 32, 32)
        for k in range(3):
            pf[u, k, rows, span] += r2[u, 0, k, :, span].astype(F32) + r2[u, 1, k, :, span].astype(F32)
        copy_of(u, q, 6).start()

        @pl.when(outer)
        def _():
            across = pl.ds(y * 32 + (1 - z // 2) * 16, 16)
            for k in range(3):
                zs[u, k, :, span] = pf[u, k, across, span].astype(BF16)
            copy_of(u, q, 7).start()

    def sum_pair(u, q):
        @pl.when(inner)
        def _():
            span = pl.ds(*SPANS[q])
            across = pl.ds(y * 32 + (1 - z // 2) * 16, 16)
            copy_of(u, q, 7).wait_recv()
            for k in range(3):
                pf[u, k, across, span] += zx[u, k, :, span].astype(F32)
            for kind in (8, 9):
                copy_of(u, q, kind).start()

    def units(u, q):
        for kind in (6, 8):
            copy_of(u, q, kind).wait_recv()
        rows, cols = piece(z, q)
        half_span = pl.ds(SPANS[q][0] // 2, SPANS[q][1] // 2)
        gate, up, grad = (
            pf[u, k, rows, cols] + (zr[u, 0, k, :, half_span] + zr[u, 1, k, :, half_span]) for k in range(3)
        )
        s = jax.nn.sigmoid(gate)
        agb[u, 0, rows, cols] = (gate * s * up).astype(BF16)
        agb[u, 1, rows, cols] = (grad * up * s * (1.0 + gate * (1.0 - s))).astype(BF16)
        agb[u, 2, rows, cols] = (grad * gate * s).astype(BF16)
        for kind in (10, 11, 12):
            copy_of(u, q, kind).start()

    def spread_y(u, q):
        for kind in (10, 11, 12):
            copy_of(u, q, kind).wait_recv()
        for kind in (13, 14):
            copy_of(u, q, kind).start()

    def forward_y(u, q):
        for kind in (13, 14):
            copy_of(u, q, kind).wait_recv()
            copy_of(u, q, kind + 2).start()

    def add_term(u, q):
        first, width = SPANS[q]
        span = slice(first, first + width)
        for half in range(2):
            feats = slice(half * TILE, half * TILE + TILE)
            term[u, half] += lax.dot_general(
                agb[u, 1, :, span], wg[feats, span], NT, preferred_element_type=F32
            ) + lax.dot_general(agb[u, 2, :, span], wu[feats, span], NT, preferred_element_type=F32)

    def back(u, q):
        for kind in (15, 16):
            copy_of(u, q, kind).wait_recv()

        @pl.when(taken(u, q))
        def _():
            copy_of(u, q, 18).start()

        @pl.when(jnp.logical_not(taken(u, q)))
        def _():
            add_term(u, q)

    def finish(u):
        pair_term(u).start()

    def send_terms(u):
        pair_term(u).wait_recv()
        term[u, core] += pair_t[u]
        for k in range(1, CHIPS):
            chip_term(u, k).start()

    stages = (dots, accumulate, sum_y, sum_pair, units, spread_y, forward_y, back)
    spans = len(SPANS)
    for u in range(UNITS):
        term[u] = jnp.zeros((2, TOK, TILE), F32)

    def unit_at(turn):
        u = jnp.int32(0)
        for index, (first, second) in enumerate(zip(ORDER, ORDER_LENDER)):
            u = jnp.where(turn == index, jnp.where(xx == 0, second, first), u)
        return u

    def step(t, _):
        for q_now in range(spans):
            for lag in reversed(range(len(stages))):
                q = (q_now - LAGS[lag]) % spans
                turn = t + (q_now - LAGS[lag]) // spans
                u = unit_at(turn)
                here = jnp.logical_and(turn >= 0, turn < UNITS)
                mine = jnp.logical_or(u < n, taken(u, q))
                if lag > 0:
                    mine = jnp.logical_and(mine, jnp.logical_not(lent(u, q)))

                @pl.when(jnp.logical_and(here, mine))
                def _(u=u, q=q, lag=lag):
                    stages[lag](u, q)

                if lag == len(stages) - 1 and q == spans - 1:

                    @pl.when(jnp.logical_and(here, jnp.logical_and(u < n, jnp.logical_not(any_lent(u)))))
                    def _(u=u):
                        finish(u)

        return 0

    def any_lent(u):
        found = lent(u, 0)
        for q in range(1, spans):
            found = jnp.logical_or(found, lent(u, q))
        return found

    lax.fori_loop(0, UNITS + (LAGS[-1] + spans - 1) // spans, step, 0)

    for unit in sorted({unit for unit, _ in LENT}):
        for q in range(spans):
            if (unit, q) in LENT:

                @pl.when(lent(unit, q))
                def _(unit=unit, q=q):
                    copy_of(unit, q, 18).wait_recv()
                    add_term(unit, q)

        @pl.when(any_lent(unit))
        def _(unit=unit):
            finish(unit)

    def spread_terms(u, _):
        send_terms(u)
        return 0

    lax.fori_loop(0, n, spread_terms, 0)

    def clear(u, _):
        for q in range(spans):

            @pl.when(taken(u, q))
            def _(q=q):
                copy_of(u, q, 18).wait_send()
                for kind in range(10, 17):
                    copy_of(u, q, kind).wait_send()

        agb[u] = jnp.zeros((3, TOK, WIDTH), BF16)
        return 0

    lax.fori_loop(n, UNITS, clear, 0)

    def store(i, k):
        cols = pl.ds(pl.multiple_of(i * TILE, TILE), TILE)
        if k == 2:
            return pltpu.make_async_copy(down_v.at[cols, :], down_hbm.at[cols, :], o_sem.at[k, i])
        src, dst = ((gate_v, gate_hbm), (up_v, up_hbm))[k]
        return pltpu.make_async_copy(src.at[:, cols], dst.at[:, cols], o_sem.at[k, i])

    xt[...] = xg[0].reshape(UNITS * TOK, FEAT).T

    def weights(i, _):
        cols = pl.ds(pl.multiple_of(i * TILE, TILE), TILE)
        act, dgate, dup = (agb[:, k, :, cols].reshape(UNITS * TOK, TILE) for k in range(3))
        gate_v[:, cols] = jnp.dot(xt[...], dgate, preferred_element_type=F32).astype(BF16)
        store(i, 0).start()
        up_v[:, cols] = jnp.dot(xt[...], dup, preferred_element_type=F32).astype(BF16)
        store(i, 1).start()
        down_v[cols, :] = lax.dot_general(
            act, xg[1].reshape(UNITS * TOK, FEAT), (((0,), (0,)), ((), ())), preferred_element_type=F32
        ).astype(BF16)
        store(i, 2).start()
        return 0

    lax.fori_loop(0, WIDTH // TILE, weights, 0)

    for u in range(UNITS):
        fs[u] = jnp.zeros((16, TILE), F32)

        def add(j, _, u=u):
            @pl.when(j == chip)
            def _():
                fs[u] += term[u, core, pl.ds(chip * 16, 16), :]

            @pl.when(j != chip)
            def _():
                remote(
                    hr.at[u, j], hr.at[u, j], h_send.at[u, 0], h_recv.at[u, j], device(z, y, j, core)
                ).wait_recv()
                fs[u] += hr[u, j]

            return 0

        lax.fori_loop(0, (8, 4, 2, 1)[u], add, 0)

    last = remote(
        fs.at[:, pl.ds(pl.multiple_of(other * 8, 8), 8), :], fr, a_send.at[9], a_recv.at[9], partner
    )
    last.start()
    last.wait()
    here = pl.ds(pl.multiple_of(core * TILE, TILE), TILE)
    there = pl.ds(pl.multiple_of(other * TILE, TILE), TILE)
    mine = pl.ds(pl.multiple_of(core * 8, 8), 8)
    for b in range(UNITS):
        u = UNITS - 1 - lev[b]
        in_grad[b, :, here] = fs[u, mine, :].astype(BF16)
        in_grad[b, :, there] = fr[u].astype(BF16)

    def drain(u, _):
        pair_term(u).wait_send()
        for k in range(1, CHIPS):
            chip_term(u, k).wait_send()
        return 0

    lax.fori_loop(0, n, drain, 0)

    def drain_sums(u, _):
        for q in range(spans):

            @pl.when(lent(u, q))
            def _(q=q):
                copy_of(u, q, 17).wait_send()

            @pl.when(jnp.logical_or(taken(u, q), jnp.logical_and(u < n, jnp.logical_not(lent(u, q)))))
            def _(q=q):
                for kind in range(7):
                    copy_of(u, q, kind).wait_send()

                @pl.when(outer)
                def _():
                    copy_of(u, q, 7).wait_send()

                @pl.when(inner)
                def _():
                    for kind in (8, 9):
                        copy_of(u, q, kind).wait_send()

            @pl.when(jnp.logical_and(u < n, jnp.logical_not(lent(u, q))))
            def _(q=q):
                for kind in range(10, 17):
                    copy_of(u, q, kind).wait_send()

        return 0

    lax.fori_loop(0, UNITS, drain_sums, 0)
    for i in range(WIDTH // TILE):
        for k in range(3):
            store(i, k).wait()


def exchange(levels, activations, out_grad, w_gate, w_up, w_down):
    vmem = pl.BlockSpec(memory_space=pltpu.VMEM)
    hbm = pl.BlockSpec(memory_space=pl.ANY)
    dma = pltpu.SemaphoreType.DMA
    return pl.pallas_call(
        kernel,
        out_shape=[
            jax.ShapeDtypeStruct(activations.shape, BF16),
            jax.ShapeDtypeStruct((FEAT, WIDTH), BF16),
            jax.ShapeDtypeStruct((FEAT, WIDTH), BF16),
            jax.ShapeDtypeStruct((WIDTH, FEAT), BF16),
        ],
        in_specs=[pl.BlockSpec(memory_space=pltpu.SMEM), vmem, vmem, hbm, hbm, hbm],
        out_specs=[vmem, hbm, hbm, hbm],
        scratch_shapes=[
            pltpu.VMEM((FEAT, WIDTH), BF16),
            pltpu.VMEM((FEAT, WIDTH), BF16),
            pltpu.VMEM((WIDTH, FEAT), BF16),
            pltpu.VMEM((64, FEAT), BF16),
            pltpu.VMEM((64, FEAT), BF16),
            pltpu.VMEM((2, UNITS, CHIPS, 16, FEAT), BF16),
            pltpu.VMEM((UNITS, 3, TOK, WIDTH), F32),
            pltpu.VMEM((UNITS, 3, TOK, WIDTH), BF16),
            pltpu.VMEM((UNITS, 2, 3, 16, WIDTH), BF16),
            pltpu.VMEM((UNITS, 2, 3, 32, WIDTH), BF16),
            pltpu.VMEM((UNITS, 2, 3, 16, WIDTH // 2), F32),
            pltpu.VMEM((UNITS, 3, 16, WIDTH), BF16),
            pltpu.VMEM((UNITS, 3, 16, WIDTH), BF16),
            pltpu.VMEM((UNITS, 3, TOK, WIDTH), BF16),
            pltpu.VMEM((UNITS, 2, TOK, TILE), F32),
            pltpu.VMEM((UNITS, TOK, TILE), F32),
            pltpu.VMEM((UNITS, CHIPS, 16, TILE), F32),
            pltpu.VMEM((UNITS, 16, TILE), F32),
            pltpu.VMEM((UNITS, 8, TILE), F32),
            pltpu.VMEM((FEAT, UNITS * TOK), BF16),
            pltpu.VMEM((FEAT, WIDTH), BF16),
            pltpu.VMEM((FEAT, WIDTH), BF16),
            pltpu.VMEM((WIDTH, FEAT), BF16),
            dma((3,)),
            dma((3, WIDTH // TILE)),
            dma((10,)),
            dma((10,)),
            dma((UNITS, len(SPANS), 19)),
            dma((UNITS, len(SPANS), 19)),
            dma((UNITS, 8)),
            dma((UNITS, 9)),
        ],
        compiler_params=pltpu.CompilerParams(
            collective_id=0, has_side_effects=True, vmem_limit_bytes=56 * 1024 * 1024
        ),
    )(levels, activations, out_grad, w_gate, w_up, w_down)


def body(activations, out_grad, w_gate, w_up, w_down, levels):
    return exchange(levels, activations, out_grad, w_gate, w_up, w_down)


def solution(mesh):
    placed = (
        P(None, "hidden", "dp"),
        P(None, "hidden", "dp"),
        P("dp", "hidden"),
        P("dp", "hidden"),
        P("hidden", "dp"),
        P(),
    )
    return jax.shard_map(
        body,
        mesh=mesh,
        in_specs=placed,
        out_specs=(
            P(None, "hidden", "dp"),
            P("dp", "hidden"),
            P("dp", "hidden"),
            P("hidden", "dp"),
        ),
        check_vma=False,
    )
```

time: 175 us -> 132 us (0.75); the launches traced: 173 us -> 132 us
  Pallas kernels: 163 us -> 123 us
  matrix products: 8.94 us -> 0 us
  local copies, waits for them, and re-layouts: 0.63 us -> 7.75 us
    pallas_call x1, Pallas kernels: 163 us -> 123 us  [exchange(): pl.pallas_call(kernel, out_shape=[jax.ShapeDtypeStruct(activations.shape,...]
    dot_general x3 -> x0, matrix products: 8.94 us -> none  [the longest x1 4.18 us: body(): dot(rows_x, dgate).astype(BF16)]
    unnamed x11 -> x8, local copies, waits for them, and re-layouts: 0.63 us -> 7.75 us
where the time goes in v2:
time: 132 us
  Pallas kernels  123 us (93%)
  local copies, waits for them, and re-layouts  7.75 us (6%)
    pallas_call x1, Pallas kernels, exchange(): pl.pallas_call(kernel, out_shape=[jax.ShapeDtypeStruct(activations.shape,...  123 us
    unnamed x8, local copies, waits for them, and re-layouts  7.75 us

profile of v2, /device:TPU:1, one launch (start us, length us, event | category | flops | bytes accessed | tf_op | source)
XLA Modules:
  0.0 131.5 jit_solution(8146528501452301866)
XLA Ops:
  0.6 123.2 %shard_map.93 = (bf16[4,8,512]{2,1,0:T(8,128)(2,1)}, bf16[512,1792]{1,0:T(8,128)(2,1)}, bf16[512,1792]{1,0:T(8,128)(2,1)}, bf16[1792,512]{1,0:T(8,128)(2,1)}) custom-call(s32[4]{0:T(128)} %lev.1, bf16[4,8,512]{2,1,0:T(8,128)(2,1)} %x_ref.1, bf16[4,8,512]{2,1,0:T(8,128)(2,1)} %g_ref.1, bf16[512,1792]{1,0:T(8,128)(2,1)} %wg_hbm.1, bf16[512,1792]{1,0:T(8,128)(2,1)} %wu_hbm.1, ...), custom_call_target="tpu_custom_call" | custom-call | tf_op jit(solution)/shard_map/pallas_call | solution.py:513
  123.8 1.4 %copy.14 = bf16[4,8,512]{2,1,0:T(8,128)(2,1)} copy(bf16[4,8,512]{2,1,0:T(8,128)(2,1)} %get-tuple-element.8) | data formatting | bytes 65536
  125.2 0.0 copy-start.1
  125.2 3.0 %copy.15 = bf16[512,1792]{1,0:T(8,128)(2,1)} copy(bf16[512,1792]{1,0:T(8,128)(2,1)} %get-tuple-element.9) | data formatting | bytes 3670016
  128.1 0.0 copy-done.1
  128.2 0.0 copy-start
  128.2 1.2 copy.16
  129.4 0.9 copy-done
  130.3 1.2 copy.17
Async XLA Ops:
  125.2 3.0 %copy-start.1 = (bf16[512,1792]{1,0:T(8,128)(2,1)S(1)}, bf16[512,1792]{1,0:T(8,128)(2,1)}, u32[]{:S(2)}) copy-start(bf16[512,1792]{1,0:T(8,128)(2,1)} %get-tuple-element.10) | copy-start | bytes 5505028
  128.2 2.2 %copy-start = (bf16[1792,512]{1,0:T(8,128)(2,1)S(1)}, bf16[1792,512]{1,0:T(8,128)(2,1)}, u32[]{:S(2)}) copy-start(bf16[1792,512]{1,0:T(8,128)(2,1)} %get-tuple-element.11) | copy-start | bytes 5505028

commit v3 on v2

--- a/solution.py
+++ b/solution.py
@@ -15,12 +15,13 @@
 WIDTH = 1792
 TILE = 256
 CHIPS = 8
-SPANS = ((0, 512), (512, 512), (1024, 768))
-LENT = {(3, 0): 1, (3, 1): 3, (3, 2): 2}
+SPANS = ((0, 256), (256, 256), (512, 256), (768, 256), (1024, 256), (1280, 256), (1536, 256))
+LENT = {(3, 0): 1, (3, 1): 3, (3, 2): 2, (3, 3): 1, (3, 4): 3, (3, 5): 2, (3, 6): 3, (2, 0): 1, (2, 1): 3}
 NT = (((1,), (1,)), ((), ()))
+COPIES = 4
 ORDER_LENDER = (3, 2, 1, 0)
-ORDER = (0, 3, 1, 2)
-LAGS = (0, 2, 4, 6, 8, 10, 12, 14)
+ORDER = (0, 3, 2, 1)
+LAGS = (0, 3, 6, 9, 12, 15, 18, 21)
 
 
 def device(z, y, chip, core):
@@ -82,39 +83,60 @@
 
     pl.semaphore_wait(barrier, len(greeted))
 
-    pair_copy = remote(own, pair, a_send.at[0], a_recv.at[0], partner)
-    pair_copy.start()
-    pair_copy.wait()
-    for u in range(0, UNITS, 2):
-        rows = pl.ds(pl.multiple_of(core * 32 + u * 8, 16), 16)
+    far = 2 * xx + (1 - zh)
+
+    def pair_copy(part):
+        rows = pl.ds(pl.multiple_of(other * 32 + part * 16, 16), 16)
+        return remote(own.at[rows], pair.at[rows], a_send.at[part, 0], a_recv.at[part, 0], partner)
+
+    def block(part, c):
+        return xg.at[core, pl.ds(part * 2, 2), c]
+
+    def gather_z(part):
+        ref = block(part, chip)
+        return remote(ref, ref, a_send.at[part, 1], a_recv.at[part, 1], device(z, y, far, core))
+
+    def gather_x(part, c, k, slot):
+        ref = block(part, c)
+        target = device(z, y, 2 * ((xx + k) % 4) + zh, core)
+        return remote(ref, ref, a_send.at[part, slot], a_recv.at[part, slot], target)
+
+    def swap(part):
+        ref = xg.at[core, pl.ds(part * 2, 2)]
+        return remote(ref, ref, a_send.at[part, 8], a_recv.at[part, 8], partner)
+
+    for part in (1, 0):
+        pair_copy(part).start()
+    for part in (1, 0):
+        pair_copy(part).wait_recv()
+        rows = pl.ds(pl.multiple_of(core * 32 + part * 16, 16), 16)
         mine, theirs = own[rows].astype(F32), pair[rows].astype(F32)
         zero = jnp.where(core == 0, mine, theirs)
         one = jnp.where(core == 0, theirs, mine)
-        xg[core, u, chip] = jnp.concatenate([zero[:8], one[:8]], 0).astype(BF16)
-        xg[core, u + 1, chip] = jnp.concatenate([zero[8:], one[8:]], 0).astype(BF16)
-
-    def block(c):
-        return xg.at[core, :, c]
-
-    far = 2 * xx + (1 - zh)
-    spread = [remote(block(chip), block(chip), a_send.at[1], a_recv.at[1], device(z, y, far, core))]
-    for k in (1, 2, 3):
-        target = device(z, y, 2 * ((xx + k) % 4) + zh, core)
-        spread.append(remote(block(chip), block(chip), a_send.at[1 + k], a_recv.at[1 + k], target))
-    for copy in spread:
-        copy.start()
-    spread[0].wait_recv()
-    for k in (1, 2, 3):
-        target = device(z, y, 2 * ((xx + k) % 4) + zh, core)
-        spread.append(remote(block(far), block(far), a_send.at[4 + k], a_recv.at[4 + k], target))
-        spread[-1].start()
-    for copy in spread[1:]:
-        copy.wait_recv()
-    for copy in spread:
-        copy.wait_send()
-    swap = remote(xg.at[core], xg.at[core], a_send.at[8], a_recv.at[8], partner)
-    swap.start()
-    swap.wait()
+        xg[core, 2 * part, chip] = jnp.concatenate([zero[:8], one[:8]], 0).astype(BF16)
+        xg[core, 2 * part + 1, chip] = jnp.concatenate([zero[8:], one[8:]], 0).astype(BF16)
+        gather_z(part).start()
+        for k in (1, 2, 3):
+            gather_x(part, chip, k, 1 + k).start()
+    for part in (1, 0):
+        gather_z(part).wait_recv()
+        for k in (1, 2, 3):
+            gather_x(part, far, k, 4 + k).start()
+
+    def start_swap(part):
+        for k in (1, 2, 3):
+            gather_x(part, chip, k, 1 + k).wait_recv()
+            gather_x(part, far, k, 4 + k).wait_recv()
+        swap(part).start()
+
+    start_swap(1)
+
+    @pl.when(xx != 0)
+    def _():
+        start_swap(0)
+        swap(0).wait_recv()
+
+    swap(1).wait_recv()
     for load in loads:
         load.wait()
 
@@ -221,6 +243,15 @@
             return 0
 
         first, width = SPANS[q]
+        if q == 0:
+
+            @pl.when(jnp.logical_and(xx == 0, u == UNITS - 2))
+            def _():
+                start_swap(0)
+
+            @pl.when(jnp.logical_and(xx == 0, u == 1))
+            def _():
+                swap(0).wait_recv()
 
         @pl.when(u < n)
         def _():
@@ -452,7 +483,7 @@
         lax.fori_loop(0, (8, 4, 2, 1)[u], add, 0)
 
     last = remote(
-        fs.at[:, pl.ds(pl.multiple_of(other * 8, 8), 8), :], fr, a_send.at[9], a_recv.at[9], partner
+        fs.at[:, pl.ds(pl.multiple_of(other * 8, 8), 8), :], fr, a_send.at[0, 9], a_recv.at[0, 9], partner
     )
     last.start()
     last.wait()
@@ -471,6 +502,13 @@
         return 0
 
     lax.fori_loop(0, n, drain, 0)
+    for part in (1, 0):
+        pair_copy(part).wait_send()
+        gather_z(part).wait_send()
+        for k in (1, 2, 3):
+            gather_x(part, chip, k, 1 + k).wait_send()
+            gather_x(part, far, k, 4 + k).wait_send()
+        swap(part).wait_send()
 
     def drain_sums(u, _):
         for q in range(spans):
@@ -546,8 +584,8 @@
             pltpu.VMEM((WIDTH, FEAT), BF16),
             dma((3,)),
             dma((3, WIDTH // TILE)),
-            dma((10,)),
-            dma((10,)),
+            dma((2, 10)),
+            dma((2, 10)),
             dma((UNITS, len(SPANS), 19)),
             dma((UNITS, len(SPANS), 19)),
             dma((UNITS, 8)),
@@ -559,8 +597,41 @@
     )(levels, activations, out_grad, w_gate, w_up, w_down)
 
 
+def settle_kernel(*refs):
+    sources, results, stages, sem = refs[:4], refs[4:8], refs[8:12], refs[12]
+    loads, stores = [], []
+    for src, stage, dst in zip(sources, stages, results):
+        pieces = 1 if src.shape[0] == UNITS else COPIES
+        size = src.shape[0] // pieces
+        for i in range(pieces):
+            rows = pl.ds(i * size, size)
+            loads.append(pltpu.make_async_copy(src.at[rows], stage.at[rows], sem.at[0, len(loads)]))
+            stores.append(pltpu.make_async_copy(stage.at[rows], dst.at[rows], sem.at[1, len(stores)]))
+    for load in loads:
+        load.start()
+    for load, store in zip(loads, stores):
+        load.wait()
+        store.start()
+    for store in stores:
+        store.wait()
+
+
+def settle(*arrays):
+    hbm = pl.BlockSpec(memory_space=pl.ANY)
+    return pl.pallas_call(
+        settle_kernel,
+        out_shape=[jax.ShapeDtypeStruct(array.shape, array.dtype) for array in arrays],
+        in_specs=[hbm] * 4,
+        out_specs=[hbm] * 4,
+        scratch_shapes=[pltpu.VMEM(array.shape, array.dtype) for array in arrays]
+        + [pltpu.SemaphoreType.DMA((2, 1 + 3 * COPIES))],
+        compiler_params=pltpu.CompilerParams(vmem_limit_bytes=60 * 1024 * 1024),
+        cost_estimate=pl.CostEstimate(flops=0, bytes_accessed=2 * 5570560, transcendentals=0),
+    )(*arrays)
+
+
 def body(activations, out_grad, w_gate, w_up, w_down, levels):
-    return exchange(levels, activations, out_grad, w_gate, w_up, w_down)
+    return settle(*exchange(levels, activations, out_grad, w_gate, w_up, w_down))
 
 
 def solution(mesh):

time: 132 us -> 122 us (0.924)
  local copies, waits for them, and re-layouts: 7.75 us -> 0 us
  Pallas kernels: 123 us -> 121 us
    unnamed x8 -> x0, local copies, waits for them, and re-layouts: 7.75 us -> none
    pallas_call x1, Pallas kernels: 123 us -> 116 us  [exchange(): pl.pallas_call(kernel, out_shape=[jax.ShapeDtypeStruct(activations.shape,...]
    pallas_call x0 -> x1, Pallas kernels: none -> 5.05 us  [settle(): pl.pallas_call(settle_kernel, out_shape=[jax.ShapeDtypeStruct(array.shape...]
where the time goes in v3:
time: 122 us
  Pallas kernels  121 us (99%)
    pallas_call x1, Pallas kernels, exchange(): pl.pallas_call(kernel, out_shape=[jax.ShapeDtypeStruct(activations.shape,...  116 us
    pallas_call x1, Pallas kernels, settle(): pl.pallas_call(settle_kernel, out_shape=[jax.ShapeDtypeStruct(array.shape...  5.05 us

profile of v3, /device:TPU:1, one launch (start us, length us, event | category | flops | bytes accessed | tf_op | source)
XLA Modules:
  0.0 122.0 jit_solution(10593987194832456069)
XLA Ops:
  0.6 116.3 %shard_map.93 = (bf16[4,8,512]{2,1,0:T(8,128)(2,1)}, bf16[512,1792]{1,0:T(8,128)(2,1)}, bf16[512,1792]{1,0:T(8,128)(2,1)}, bf16[1792,512]{1,0:T(8,128)(2,1)}) custom-call(s32[4]{0:T(128)} %lev.1, bf16[4,8,512]{2,1,0:T(8,128)(2,1)} %x_ref.1, bf16[4,8,512]{2,1,0:T(8,128)(2,1)} %g_ref.1, bf16[512,1792]{1,0:T(8,128)(2,1)} %wg_hbm.1, bf16[512,1792]{1,0:T(8,128)(2,1)} %wu_hbm.1, ...), custom_call_target="tpu_custom_call" | custom-call | tf_op jit(solution)/shard_map/pallas_call | solution.py:551
  116.9 5.1 %shard_map.94 = (bf16[4,8,512]{2,1,0:T(8,128)(2,1)}, bf16[512,1792]{1,0:T(8,128)(2,1)}, bf16[512,1792]{1,0:T(8,128)(2,1)}, bf16[1792,512]{1,0:T(8,128)(2,1)}) custom-call(bf16[4,8,512]{2,1,0:T(8,128)(2,1)} %get-tuple-element.8.refs_0_, bf16[512,1792]{1,0:T(8,128)(2,1)} %get-tuple-element.9.refs_1_, bf16[512,1792]{1,0:T(8,128)(2,1)} %get-tuple-element.10.refs_2_, ...), custom_call_target="tpu_custom_call" | custom-call | bytes 11141120 | tf_op jit(solution)/shard_map/pallas_call | solution.py:621

commit v4 on v3

--- a/solution.py
+++ b/solution.py
@@ -18,6 +18,7 @@
 SPANS = ((0, 256), (256, 256), (512, 256), (768, 256), (1024, 256), (1280, 256), (1536, 256))
 LENT = {(3, 0): 1, (3, 1): 3, (3, 2): 2, (3, 3): 1, (3, 4): 3, (3, 5): 2, (3, 6): 3, (2, 0): 1, (2, 1): 3}
 NT = (((1,), (1,)), ((), ()))
+COLLECT = (1, 4)
 COPIES = 4
 ORDER_LENDER = (3, 2, 1, 0)
 ORDER = (0, 3, 2, 1)
@@ -80,6 +81,9 @@
             rows.append(ref[index].astype(F32))
         own[array * 32 : array * 32 + 16] = jnp.concatenate(rows[:2], 0).astype(BF16)
         own[array * 32 + 16 : array * 32 + 32] = jnp.concatenate(rows[2:], 0).astype(BF16)
+
+    for u in range(UNITS):
+        term[u] = jnp.zeros((2, TOK, TILE), F32)
 
     pl.semaphore_wait(barrier, len(greeted))
 
@@ -366,8 +370,6 @@
 
     stages = (dots, accumulate, sum_y, sum_pair, units, spread_y, forward_y, back)
     spans = len(SPANS)
-    for u in range(UNITS):
-        term[u] = jnp.zeros((2, TOK, TILE), F32)
 
     def unit_at(turn):
         u = jnp.int32(0)
@@ -375,8 +377,35 @@
             u = jnp.where(turn == index, jnp.where(xx == 0, second, first), u)
         return u
 
+    turns = UNITS + (LAGS[-1] + spans - 1) // spans
+    lent_units = sorted({unit for unit, _ in LENT}, reverse=True)
+
+    def collect(unit):
+        for q in range(spans):
+            if (unit, q) in LENT:
+
+                @pl.when(lent(unit, q))
+                def _(unit=unit, q=q):
+                    copy_of(unit, q, 18).wait_recv()
+                    add_term(unit, q)
+
+        @pl.when(any_lent(unit))
+        def _():
+            finish(unit)
+
     def step(t, _):
+        @pl.when(t == turns - 2)
+        def _():
+            xt[...] = xg[0].reshape(UNITS * TOK, FEAT).T
+
         for q_now in range(spans):
+            for unit, place in zip(lent_units, COLLECT):
+                if q_now == place:
+
+                    @pl.when(t == turns - 1)
+                    def _(unit=unit):
+                        collect(unit)
+
             for lag in reversed(range(len(stages))):
                 q = (q_now - LAGS[lag]) % spans
                 turn = t + (q_now - LAGS[lag]) // spans
@@ -404,23 +433,10 @@
             found = jnp.logical_or(found, lent(u, q))
         return found
 
-    lax.fori_loop(0, UNITS + (LAGS[-1] + spans - 1) // spans, step, 0)
-
-    for unit in sorted({unit for unit, _ in LENT}):
-        for q in range(spans):
-            if (unit, q) in LENT:
-
-                @pl.when(lent(unit, q))
-                def _(unit=unit, q=q):
-                    copy_of(unit, q, 18).wait_recv()
-                    add_term(unit, q)
-
-        @pl.when(any_lent(unit))
-        def _(unit=unit):
-            finish(unit)
-
-    def spread_terms(u, _):
-        send_terms(u)
+    lax.fori_loop(0, turns, step, 0)
+
+    def spread_terms(i, _):
+        send_terms(n - 1 - i)
         return 0
 
     lax.fori_loop(0, n, spread_terms, 0)
@@ -445,8 +461,6 @@
             return pltpu.make_async_copy(down_v.at[cols, :], down_hbm.at[cols, :], o_sem.at[k, i])
         src, dst = ((gate_v, gate_hbm), (up_v, up_hbm))[k]
         return pltpu.make_async_copy(src.at[:, cols], dst.at[:, cols], o_sem.at[k, i])
-
-    xt[...] = xg[0].reshape(UNITS * TOK, FEAT).T
 
     def weights(i, _):
         cols = pl.ds(pl.multiple_of(i * TILE, TILE), TILE)

time: 122 us -> 122 us (level)
  no operation moved by 1% of the time
where the time goes in v4:
time: 122 us
  Pallas kernels  121 us (99%)
    pallas_call x1, Pallas kernels, exchange(): pl.pallas_call(kernel, out_shape=[jax.ShapeDtypeStruct(activations.shape,...  116 us
    pallas_call x1, Pallas kernels, settle(): pl.pallas_call(settle_kernel, out_shape=[jax.ShapeDtypeStruct(array.shape...  5.05 us

profile of v4, /device:TPU:1, one launch (start us, length us, event | category | flops | bytes accessed | tf_op | source)
XLA Modules:
  0.0 121.8 jit_solution(8703747234078152968)
XLA Ops:
  0.6 116.1 %shard_map.93 = (bf16[4,8,512]{2,1,0:T(8,128)(2,1)}, bf16[512,1792]{1,0:T(8,128)(2,1)}, bf16[512,1792]{1,0:T(8,128)(2,1)}, bf16[1792,512]{1,0:T(8,128)(2,1)}) custom-call(s32[4]{0:T(128)} %lev.1, bf16[4,8,512]{2,1,0:T(8,128)(2,1)} %x_ref.1, bf16[4,8,512]{2,1,0:T(8,128)(2,1)} %g_ref.1, bf16[512,1792]{1,0:T(8,128)(2,1)} %wg_hbm.1, bf16[512,1792]{1,0:T(8,128)(2,1)} %wu_hbm.1, ...), custom_call_target="tpu_custom_call" | custom-call | tf_op jit(solution)/shard_map/pallas_call | solution.py:565
  116.7 5.1 %shard_map.94 = (bf16[4,8,512]{2,1,0:T(8,128)(2,1)}, bf16[512,1792]{1,0:T(8,128)(2,1)}, bf16[512,1792]{1,0:T(8,128)(2,1)}, bf16[1792,512]{1,0:T(8,128)(2,1)}) custom-call(bf16[4,8,512]{2,1,0:T(8,128)(2,1)} %get-tuple-element.8.refs_0_, bf16[512,1792]{1,0:T(8,128)(2,1)} %get-tuple-element.9.refs_1_, bf16[512,1792]{1,0:T(8,128)(2,1)} %get-tuple-element.10.refs_2_, ...), custom_call_target="tpu_custom_call" | custom-call | bytes 11141120 | tf_op jit(solution)/shard_map/pallas_call | solution.py:635
